TPU v7x, 32 devices: a whole 2x2x4 slice. The times are simulated.
32 devices in a mesh: groups: 2 (over x), goal: 16 (over z, y, core).
Axes of the slice: x: 2, y: 2, z: 4, core: 2. Of those that a mesh axis runs over, the one named last changes fastest.
Arguments:
- queries: bfloat16 [128, 64, 4096], P(('groups', 'goal')), parts along dimension 0, may hold values from -8 to 8
- goal_keys: bfloat16 [32, 256, 4096], P(('groups', 'goal')), parts along dimension 0, may hold values from -8 to 8
- goal_values: bfloat16 [32, 256, 4096], P(('groups', 'goal')), parts along dimension 0, may hold values from -6 to 6
- out_weight: bfloat16 [4096, 2048], P('goal'), may hold values from -0.5 to 0.5
- tactic_goal: int32 [128, 1], P(('groups', 'goal')), parts along dimension 0, may hold values from 0 to 15
- tactic_len: int32 [128], P(('groups', 'goal')), parts along dimension 0, may hold values from 1 to 64
Outputs:
- projected: bfloat16 [128, 64, 2048], P(('groups', 'goal')), parts along dimension 0
There are 2 independent parts, one for each index of `groups`. A program takes and returns all parts, laid end to end along the dimension named above; an argument that names none is the same for every part. Nothing has to cross between parts.
Inputs may be any that keep to these rules, and one draw needn't show every extreme that they name: `tactic_goal`: every goal is read by at least one tactic; tactics per goal are uneven. `tactic_len`: the live positions of a tactic are its leading ones.
All inputs are finite; a program needn't handle non-finite values.
Results may differ from a plain program's by a relative error of at most 0.01.
Values may be sent and summed in bfloat16 or wider, within the bound.
A program may use at most 192 MiB of HBM per device.

v0:
```python
import math
import jax
import jax.numpy as jnp
from jax import lax
from jax.sharding import PartitionSpec as P

DH = 64


def attend_block(query_block, keys_heads, values_heads, block_ids):
    tact_count = query_block.shape[0]
    row_count = query_block.shape[1]
    width_local = query_block.shape[2]
    head_count = width_local // DH
    keys_tact = jnp.take(keys_heads, block_ids, axis=0).reshape(tact_count, -1, head_count, DH)
    vals_tact = jnp.take(values_heads, block_ids, axis=0).reshape(tact_count, -1, head_count, DH)
    query_four = query_block.reshape(tact_count, row_count, head_count, DH)
    scores = jnp.einsum(
        "tihd,tjhd->thij", query_four, keys_tact, preferred_element_type=jnp.float32
    )
    biggest = jnp.max(scores, axis=-1, keepdims=True)
    powers = jnp.exp(scores - biggest)
    weights = (powers / jnp.sum(powers, axis=-1, keepdims=True)).astype(jnp.bfloat16)
    attended = jnp.einsum("thij,tjhd->tihd", weights, vals_tact, preferred_element_type=jnp.float32)
    return attended.reshape(tact_count, row_count, width_local).astype(jnp.bfloat16)


def attend(query_piece, keys_heads, values_heads, goal_ids):
    tact_count = query_piece.shape[0]
    row_count = query_piece.shape[1]
    width_local = query_piece.shape[2]
    block_size = math.gcd(tact_count, 64)
    block_count = tact_count // block_size
    query_blocks = query_piece.reshape(block_count, block_size, row_count, width_local)
    id_blocks = goal_ids.reshape(block_count, block_size)

    def one_block(operands):
        return attend_block(operands[0], keys_heads, values_heads, operands[1])

    results = lax.map(one_block, (query_blocks, id_blocks))
    return results.reshape(tact_count, row_count, width_local)


def shards(queries, goal_keys, goal_values, out_weight, tactic_goal, tactic_len):
    goal_ids = lax.all_gather(tactic_goal[:, 0], "goal", axis=0, tiled=True)
    keys_heads, values_heads = (
        lax.all_to_all(goal_keys, "goal", split_axis=2, concat_axis=0, tiled=True),
        lax.all_to_all(goal_values, "goal", split_axis=2, concat_axis=0, tiled=True),
    )
    query_heads = lax.all_to_all(queries, "goal", split_axis=2, concat_axis=0, tiled=True)
    attended = attend(query_heads, keys_heads, values_heads, goal_ids)
    merged = lax.all_to_all(attended, "goal", split_axis=0, concat_axis=2, tiled=True)
    live_rows = jnp.arange(merged.shape[1])[None, :] < tactic_len[:, None]
    context = jnp.where(live_rows[:, :, None], merged, jnp.zeros_like(merged))
    tact_local = context.shape[0]
    row_count = context.shape[1]
    flat = context.reshape(tact_local * row_count, context.shape[2])
    projected = jnp.dot(
        flat,
        lax.all_gather(out_weight, "goal", axis=0, tiled=True),
        preferred_element_type=jnp.float32,
    )
    return projected.astype(jnp.bfloat16).reshape(tact_local, row_count, out_weight.shape[1])


def solution(mesh):
    return jax.shard_map(
        shards,
        mesh=mesh,
        in_specs=(
            P(("groups", "goal"), None, None),
            P(("groups", "goal"), None, None),
            P(("groups", "goal"), None, None),
            P("goal", None),
            P(("groups", "goal"), None),
            P(("groups", "goal")),
        ),
        out_specs=P(("groups", "goal"), None, None),
        check_vma=False,
    )
```

profile of v0, /device:TPU:13, one launch (start us, length us, event | category | flops | bytes accessed | tf_op | source)
XLA Modules:
  0.0 509.1 jit_solution(2314349538631211243)
XLA Ops:
  7.3 10.1 %copy.23 = bf16[1,256,4096]{1,0,2:T(2,128)(2,1)} copy(bf16[1,256,4096]{2,1,0:T(8,128)(2,1)} %param.10) | data formatting | bytes 4194304 | tf_op args[2]
  17.8 21.7 %reduce.1 = bf16[4096,256]{1,0:T(8,128)(2,1)S(1)} reduce(bf16[4096,1,256]{2,1,0:T(2,128)(2,1)} %bitcast.58, bf16[]{:T(256)} %broadcast.32), dimensions={1}, to_apply=%bitcast.44.reduce_sub_computation | reduce | bytes 4194306
  41.6 6.6 %all-to-all-start = ((bf16[16,2,32768]{2,1,0:T(2,128)(2,1)}), bf16[16,2,32768]{2,1,0:T(2,128)(2,1)S(1)}, u32[]{:S(2)}, u32[]{:S(2)}) async-start(bf16[16,2,32768]{2,1,0:T(2,128)(2,1)} %reshape.91), calls=%async_computation | async-start | bytes 4194304 | tf_op jit(solution)/shard_map/all_to_all | solution.py:48
  48.1 10.1 %copy.26 = bf16[1,256,4096]{1,0,2:T(2,128)(2,1)} copy(bf16[1,256,4096]{2,1,0:T(8,128)(2,1)} %param.9) | data formatting | bytes 4194304 | tf_op args[1]
  58.2 23.0 %reduce = bf16[4096,256]{1,0:T(8,128)(2,1)} reduce(bf16[4096,1,256]{2,1,0:T(2,128)(2,1)} %bitcast.59, bf16[]{:T(256)} %broadcast.32), dimensions={1}, to_apply=%bitcast.46.reduce_sub_computation | reduce | bytes 4194306
  81.1 4.0 reshape.93
  85.1 58.2 %all-to-all-done = bf16[16,2,32768]{2,1,0:T(2,128)(2,1)S(1)} async-done(((bf16[16,2,32768]{2,1,0:T(2,128)(2,1)}), bf16[16,2,32768]{2,1,0:T(2,128)(2,1)S(1)}, u32[]{:S(2)}, u32[]{:S(2)}) %all-to-all-start) | async-done | bytes 2097184 | tf_op jit(solution)/shard_map/all_to_all | solution.py:48
  143.3 4.3 all-to-all-start.1
  147.7 7.0 %copy.29 = bf16[4,64,4096]{1,0,2:T(4,128)(2,1)} copy(bf16[4,64,4096]{2,1,0:T(8,128)(2,1)} %param.8) | data formatting | bytes 4194304 | tf_op args[0]
  154.7 7.5 %reshape.95 = bf16[16,2,32768]{2,1,0:T(2,128)(2,1)} reshape(bf16[4096,4,64]{2,1,0:T(4,128)(2,1)} %bitcast.63) | data formatting | bytes 4194304
  162.3 52.0 %all-to-all-done.1 = bf16[16,2,32768]{2,1,0:T(2,128)(2,1)} async-done(((bf16[16,2,32768]{2,1,0:T(2,128)(2,1)}), bf16[16,2,32768]{2,1,0:T(2,128)(2,1)}, u32[]{:S(2)}, u32[]{:S(2)}) %all-to-all-start.1) | async-done | bytes 2097184 | tf_op jit(solution)/shard_map/all_to_all | solution.py:47
  214.3 4.7 all-to-all-start.2
  220.4 44.1 %all-reduce = s32[64]{0:T(128)S(1)} all-reduce(s32[64]{0:T(128)S(1)} %bitcast_dynamic-update-slice_fusion), channel_id=2, replica_groups=mesh['groups'=2,'goal'=16] {'goal'}, use_global_device_ids=true, to_apply=%add | all-reduce | flops 64 | bytes 512 | tf_op jit(solution)/shard_map/all_gather | solution.py:45
  264.5 6.8 %reshape.92 = bf16[4096,1,256]{2,1,0:T(2,128)(2,1)} reshape(bf16[16,2,32768]{2,1,0:T(2,128)(2,1)S(1)} %all-to-all-done) | data formatting | bytes 4194304
  271.3 3.9 copy.34
  278.0 10.5 %reshape.94 = bf16[4096,1,256]{2,1,0:T(2,128)(2,1)} reshape(bf16[16,2,32768]{2,1,0:T(2,128)(2,1)} %all-to-all-done.1) | data formatting | bytes 4194304
  288.5 3.9 copy.35
  292.4 3.9 copy.27
  296.3 5.5 %gather_fusion = bf16[64,256,256]{2,1,0:T(8,128)(2,1)} fusion(bf16[16,256,256]{2,1,0:T(8,128)(2,1)S(1)} %bitcast.56, s32[1024]{0:T(1024)S(1)} %pad_clamp_fusion), kind=kCustom, calls=%fused_computation.clone | custom fusion | bytes 16777472 | tf_op jit(solution)/shard_map/while/body/eval_jaxpr/jit(_take)/gather | solution.py:16
  301.8 7.1 %gather_fusion.1 = bf16[64,256,256]{2,1,0:T(8,128)(2,1)} fusion(bf16[16,256,256]{2,1,0:T(8,128)(2,1)} %bitcast.57, s32[1024]{0:T(1024)S(1)} %pad_clamp_fusion), kind=kCustom, calls=%fused_computation.1.clone | custom fusion | bytes 16777472 | tf_op jit(solution)/shard_map/while/body/eval_jaxpr/jit(_take)/gather | solution.py:15
  308.9 11.6 %broadcast_select_fusion = (bf16[64,256,256]{2,1,0:T(8,128)(2,1)}, bf16[64,256,256]{2,1,0:T(8,128)(2,1)}) fusion(bf16[64,256,256]{2,1,0:T(8,128)(2,1)} %gather_fusion.1, pred[64]{0:T(512)(128)(4,1)S(1)} %compare_and_fusion, bf16[64,256,256]{2,1,0:T(8,128)(2,1)} %gather_fusion), kind=kLoop, calls=%fused_computation.9 | loop fusion | flops 8388608 | bytes 33554496 | tf_op jit(solution)/shard_map/while/body/eval_jaxpr/jit(_take)/select_n | solution.py:15
  320.5 11.9 %copy.28 = bf16[64,256,256]{1,2,0:T(8,128)(2,1)} copy(bf16[64,256,256]{2,1,0:T(8,128)(2,1)} %get-tuple-element.16) | data formatting | bytes 16777216 | tf_op jit(solution)/shard_map/while/body/eval_jaxpr/jit(_take)/select_n | solution.py:15
  332.4 7.5 %reshape.96 = bf16[4096,4,64]{2,1,0:T(4,128)(2,1)} reshape(bf16[16,2,32768]{2,1,0:T(2,128)(2,1)} %all-to-all-done.2) | data formatting | bytes 4194304
  339.9 5.4 %copy.30 = bf16[4,64,16,256]{3,1,0,2:T(8,128)(2,1)S(1)} copy(bf16[4,64,16,256]{1,0,3,2:T(4,128)(2,1)} %bitcast.62) | data formatting | bytes 4194304 | tf_op jit(solution)/shard_map/all_to_all | solution.py:50
  348.5 11.9 %copy.25 = bf16[64,256,256]{1,2,0:T(8,128)(2,1)} copy(bf16[64,256,256]{2,1,0:T(8,128)(2,1)} %get-tuple-element.17) | data formatting | bytes 16777216 | tf_op jit(solution)/shard_map/while/body/eval_jaxpr/jit(_take)/select_n | solution.py:16
  360.4 12.7 %fusion.6 = f32[64,4,256,64]{2,3,1,0:T(8,128)} fusion(bf16[64,256,4,64]{1,3,2,0:T(8,128)(2,1)} %bitcast.55, bf16[64,64,4,64]{3,2,1,0:T(4,128)(2,1)} %reshape.60), kind=kOutput, calls=%fused_computation.11 | convolution fusion | flops 536870912 | bytes 27262976 | tf_op jit(solution)/shard_map/while/body/eval_jaxpr/tihd,tjhd->thij/dot_general | solution.py:18
  373.1 14.6 %fusion.18 = f32[64,4,64]{2,1,0:T(4,128)S(1)} fusion(f32[64,4,256,64]{2,3,1,0:T(8,128)} %fusion.6), kind=kOutput, calls=%fused_computation.25 | output fusion | flops 8388863 | bytes 16842752 | tf_op jit(solution)/shard_map/while/body/eval_jaxpr/sub | solution.py:22
  387.7 43.3 %fusion.8 = bf16[64,4,64,64]{3,2,1,0:T(8,128)(2,1)} fusion(bf16[64,256,4,64]{1,3,2,0:T(8,128)(2,1)} %bitcast.67, f32[64,4,64]{2,1,0:T(4,128)S(1)} %fusion.18, f32[64,4,256,64]{2,3,1,0:T(8,128)} %fusion.6), kind=kOutput, calls=%fused_computation.13 | convolution fusion | flops 550519040 | bytes 27328512 | tf_op jit(solution)/shard_map/while/body/eval_jaxpr/thij,tjhd->tihd/dot_general | solution.py:24
  431.1 4.8 copy.32
  435.9 7.5 %all-to-all-start.3 = ((bf16[64,64,256]{2,1,0:T(8,128)(2,1)}), bf16[64,64,256]{2,1,0:T(8,128)(2,1)S(1)}, u32[]{:S(2)}, u32[]{:S(2)}) async-start(bf16[64,64,256]{2,1,0:T(8,128)(2,1)} %copy.32), calls=%async_computation.3 | async-start | bytes 4194304 | tf_op jit(solution)/shard_map/all_to_all | solution.py:52
  443.6 47.3 %all-to-all-done.3 = bf16[64,64,256]{2,1,0:T(8,128)(2,1)S(1)} async-done(((bf16[64,64,256]{2,1,0:T(8,128)(2,1)}), bf16[64,64,256]{2,1,0:T(8,128)(2,1)S(1)}, u32[]{:S(2)}, u32[]{:S(2)}) %all-to-all-start.3) | async-done | bytes 2097184 | tf_op jit(solution)/shard_map/all_to_all | solution.py:52
  493.0 9.3 %convolution_convert_fusion = bf16[256,2048]{1,0:T(8,128)(2,1)} fusion(bf16[4096,2048]{1,0:T(8,128)(2,1)} %all-gather.3.cloned.1.call-done, bf16[256,4096]{1,0:T(8,128)(2,1)S(1)} %bitcast.71, pred[256]{0:T(512)(128)(4,1)S(1)} %lt.30), kind=kOutput, calls=%fused_computation.14 | convolution fusion | flops 4296540160 | bytes 19923200 | tf_op jit(solution)/shard_map/dot_general | solution.py:58
  (24 shorter events, 12.4 us)
Async XLA Ops:
  6.5 486.4 %all-gather.3.cloned.1.call-start = ((), (), s32[]{:S(2)}) async-start(), calls=%async_computation.4 | async-start | bytes 17825792 | tf_op jit(solution)/shard_map/all_gather | solution.py:60
  41.6 101.8 %all-to-all-start = ((bf16[16,2,32768]{2,1,0:T(2,128)(2,1)}), bf16[16,2,32768]{2,1,0:T(2,128)(2,1)S(1)}, u32[]{:S(2)}, u32[]{:S(2)}) async-start(bf16[16,2,32768]{2,1,0:T(2,128)(2,1)} %reshape.91), calls=%async_computation | async-start | bytes 4194304 | tf_op jit(solution)/shard_map/all_to_all | solution.py:48
  143.3 71.0 %all-to-all-start.1 = ((bf16[16,2,32768]{2,1,0:T(2,128)(2,1)}), bf16[16,2,32768]{2,1,0:T(2,128)(2,1)}, u32[]{:S(2)}, u32[]{:S(2)}) async-start(bf16[16,2,32768]{2,1,0:T(2,128)(2,1)} %reshape.93), calls=%async_computation.1 | async-start | bytes 4194304 | tf_op jit(solution)/shard_map/all_to_all | solution.py:47
  147.7 71.4 %copy-start.2 = (u32[32]{0:T(128)S(1)}, u32[32]{0:T(128)}, u32[]{:S(2)}) copy-start(u32[32]{0:T(128)} %constant.37) | copy-start | bytes 388
  147.7 72.6 %copy-start = (s32[4,1]{0,1:T(1,128)S(1)}, s32[4,1]{0,1:T(1,128)}, u32[]{:S(2)}) copy-start(s32[4,1]{0,1:T(1,128)} %param.12) | copy-start | bytes 52
  214.3 118.2 %all-to-all-start.2 = ((bf16[16,2,32768]{2,1,0:T(2,128)(2,1)}), bf16[16,2,32768]{2,1,0:T(2,128)(2,1)}, u32[]{:S(2)}, u32[]{:S(2)}) async-start(bf16[16,2,32768]{2,1,0:T(2,128)(2,1)} %reshape.95), calls=%async_computation.2 | async-start | bytes 4194304 | tf_op jit(solution)/shard_map/all_to_all | solution.py:50
  431.1 12.3 %copy-start.1 = (s32[4]{0:T(128)S(1)}, s32[4]{0:T(128)}, u32[]{:S(2)}) copy-start(s32[4]{0:T(128)} %param.13) | copy-start | bytes 52
  435.9 54.9 %all-to-all-start.3 = ((bf16[64,64,256]{2,1,0:T(8,128)(2,1)}), bf16[64,64,256]{2,1,0:T(8,128)(2,1)S(1)}, u32[]{:S(2)}, u32[]{:S(2)}) async-start(bf16[64,64,256]{2,1,0:T(8,128)(2,1)} %copy.32), calls=%async_computation.3 | async-start | bytes 4194304 | tf_op jit(solution)/shard_map/all_to_all | solution.py:52
Sparse Core Ops, SparseCore 0:
  9.5 193.1 all-gather.2
where the time goes:
time: 512 us; the launch traced here: 509 us
  waiting for transfers between devices  158 us (31%)
  local copies, waits for them, and re-layouts  133 us (26%)
  other arithmetic  70.9 us (14%)
  matrix products  65.3 us (13%)
  blocking collectives  44.1 us (9%)
  starting transfers between devices  23.2 us (5%)
  between operations  14.2 us (3%)
    unnamed x22, local copies, waits for them, and re-layouts  75.4 us
    all_to_all x1, waiting for transfers between devices, shards(): lax.all_to_all(goal_values, 'goal', split_axis=2, concat_axis=0, tiled=True)  58.2 us
    all_to_all x1, waiting for transfers between devices, shards(): lax.all_to_all(goal_keys, 'goal', split_axis=2, concat_axis=0, tiled=True)  52 us
    all_to_all x1, waiting for transfers between devices, shards(): lax.all_to_all(attended, 'goal', split_axis=0, concat_axis=2, tiled=True)  47.3 us
    unnamed x2, other arithmetic  44.6 us
    all_gather x1, blocking collectives, shards(): goal_ids = lax.all_gather(tactic_goal[:, 0], 'goal', axis=0, tiled=True)  44.1 us
    dot_general x1, matrix products, attend_block(): jnp.einsum('thij,tjhd->tihd', weights, vals_tact, preferred_element_type=...  43.3 us
    sub x1, other arithmetic, attend_block(): powers = jnp.exp(scores - biggest)  14.6 us
  transfers between devices with their start and end apart: 5, of which 3 were waited for; matrix products, arithmetic and copies ran while one was open for 51% of the time, Pallas kernels for 0%

commit v1 on v0

--- a/solution.py
+++ b/solution.py
@@ -5,6 +5,29 @@
 from jax.sharding import PartitionSpec as P
 
 DH = 64
+
+
+def split_up(array, dim, size):
+    shape = array.shape
+    parts = array.reshape(*shape[:dim], size, shape[dim] // size, *shape[dim + 1 :])
+    return jnp.moveaxis(parts, dim, 0)
+
+
+def laid_out(parts, dim):
+    parts = jnp.moveaxis(parts, 0, dim)
+    shape = parts.shape
+    return parts.reshape(*shape[:dim], shape[dim] * shape[dim + 1], *shape[dim + 2 :])
+
+
+def swapped_with_each(value, axis, split_dim, concat_dim):
+    peers, index = (lax.axis_size(axis), lax.axis_index(axis))
+    tiles = split_up(value, split_dim, peers)
+    finished = [tiles[index]]
+    for hop in range(1, peers):
+        sent = tiles[index ^ hop]
+        finished.append(lax.ppermute(sent, axis, [(i, i ^ hop) for i in range(peers)]))
+    tiles = jnp.stack(finished)[index ^ jnp.arange(peers)]
+    return laid_out(tiles, concat_dim)
 
 
 def attend_block(query_block, keys_heads, values_heads, block_ids):
@@ -45,7 +68,7 @@
     goal_ids = lax.all_gather(tactic_goal[:, 0], "goal", axis=0, tiled=True)
     keys_heads, values_heads = (
         lax.all_to_all(goal_keys, "goal", split_axis=2, concat_axis=0, tiled=True),
-        lax.all_to_all(goal_values, "goal", split_axis=2, concat_axis=0, tiled=True),
+        swapped_with_each(goal_values, "goal", 2, 0),
     )
     query_heads = lax.all_to_all(queries, "goal", split_axis=2, concat_axis=0, tiled=True)
     attended = attend(query_heads, keys_heads, values_heads, goal_ids)

time: 512 us -> 490 us (0.957)
  waiting for transfers between devices: 158 us -> 103 us
  starting transfers between devices: 23.2 us -> 49.9 us
  other arithmetic: 70.9 us -> 48.1 us
  blocking collectives: 44.1 us -> 64.4 us
  local copies, waits for them, and re-layouts: 133 us -> 143 us
    all_to_all x1 -> x0, waiting for transfers between devices: 58.2 us -> none  [shards(): lax.all_to_all(goal_values, 'goal', split_axis=2, concat_axis=0, tiled=True)]
    ppermute x0 -> x15, waiting for transfers between devices: none -> 55.3 us  [swapped_with_each(): lax.ppermute(sent, axis, [(i, i ^ hop) for i in range(peers)])]
    all_to_all x1, waiting for transfers between devices: 52 us -> 0.01 us  [shards(): lax.all_to_all(goal_keys, 'goal', split_axis=2, concat_axis=0, tiled=True)]
    ppermute x0 -> x15, starting transfers between devices: none -> 32.7 us  [swapped_with_each(): lax.ppermute(sent, axis, [(i, i ^ hop) for i in range(peers)])]
    unnamed x2 -> x1, other arithmetic: 44.6 us -> 21.7 us
    all_gather x1, blocking collectives: 44.1 us -> 64.4 us  [shards(): goal_ids = lax.all_gather(tactic_goal[:, 0], 'goal', axis=0, tiled=True)]
    another operation x0 -> x18, local copies, waits for them, and re-layouts: none -> 13.2 us
    all_to_all x1 -> x0, starting transfers between devices: 6.55 us -> none  [shards(): lax.all_to_all(goal_values, 'goal', split_axis=2, concat_axis=0, tiled=True)]
  transfers between devices with their start and end apart: 5 -> 19, of which waited for: 3 -> 5; matrix products, arithmetic and copies ran while one was open for 51% -> 50% of each run, Pallas kernels for 0% -> 0%
where the time goes in v1:
time: 490 us; the launch traced here: 488 us
  local copies, waits for them, and re-layouts  143 us (29%)
  waiting for transfers between devices  103 us (21%)
  matrix products  65.2 us (13%)
  blocking collectives  64.4 us (13%)
  starting transfers between devices  49.9 us (10%)
  other arithmetic  48.1 us (10%)
  between operations  14.2 us (3%)
    unnamed x36, local copies, waits for them, and re-layouts  74.8 us
    all_gather x1, blocking collectives, shards(): goal_ids = lax.all_gather(tactic_goal[:, 0], 'goal', axis=0, tiled=True)  64.4 us
    ppermute x15, waiting for transfers between devices, swapped_with_each(): lax.ppermute(sent, axis, [(i, i ^ hop) for i in range(peers)])  55.3 us
    all_to_all x1, waiting for transfers between devices, shards(): lax.all_to_all(attended, 'goal', split_axis=0, concat_axis=2, tiled=True)  47.3 us
    dot_general x1, matrix products, attend_block(): jnp.einsum('thij,tjhd->tihd', weights, vals_tact, preferred_element_type=...  43.2 us
    ppermute x15, starting transfers between devices, swapped_with_each(): lax.ppermute(sent, axis, [(i, i ^ hop) for i in range(peers)])  32.7 us
    unnamed x1, other arithmetic  21.7 us
    sub x1, other arithmetic, attend_block(): powers = jnp.exp(scores - biggest)  14.7 us
  transfers between devices with their start and end apart: 19, of which 5 were waited for; matrix products, arithmetic and copies ran while one was open for 50% of the time, Pallas kernels for 0%

profile of v1, /device:TPU:13, one launch (start us, length us, event | category | flops | bytes accessed | tf_op | source)
XLA Modules:
  0.0 487.7 jit_solution(9988115716624123245)
XLA Ops:
  7.3 10.0 %copy.55 = bf16[1,256,4096]{1,0,2:T(2,128)(2,1)} copy(bf16[1,256,4096]{2,1,0:T(8,128)(2,1)} %param.9) | data formatting | bytes 4194304 | tf_op args[1]
  17.8 21.7 %reduce = bf16[4096,256]{1,0:T(8,128)(2,1)S(1)} reduce(bf16[4096,1,256]{2,1,0:T(2,128)(2,1)} %bitcast.102, bf16[]{:T(256)} %broadcast.67), dimensions={1}, to_apply=%bitcast.91.reduce_sub_computation | reduce | bytes 4194306
  41.5 6.6 %all-to-all-start = ((bf16[16,2,32768]{2,1,0:T(2,128)(2,1)}), bf16[16,2,32768]{2,1,0:T(2,128)(2,1)S(1)}, u32[]{:S(2)}, u32[]{:S(2)}) async-start(bf16[16,2,32768]{2,1,0:T(2,128)(2,1)} %reshape.157), calls=%async_computation | async-start | bytes 4194304 | tf_op jit(solution)/shard_map/all_to_all | solution.py:70
  48.1 4.1 copy.37
  52.1 2.5 constant_dynamic-slice_fusion
  68.9 64.4 %all-reduce = s32[64]{0:T(128)S(1)} all-reduce(s32[64]{0:T(128)S(1)} %bitcast_dynamic-update-slice_fusion.16), channel_id=2, replica_groups=mesh['groups'=2,'goal'=16] {'goal'}, use_global_device_ids=true, to_apply=%add | all-reduce | flops 64 | bytes 512 | tf_op jit(solution)/shard_map/all_gather | solution.py:68
  136.0 6.9 %copy.58 = bf16[4,64,4096]{1,0,2:T(4,128)(2,1)} copy(bf16[4,64,4096]{2,1,0:T(8,128)(2,1)} %param.8) | data formatting | bytes 4194304 | tf_op args[0]
  142.9 7.5 %reshape.159 = bf16[16,2,32768]{2,1,0:T(2,128)(2,1)} reshape(bf16[4096,4,64]{2,1,0:T(4,128)(2,1)} %bitcast.105) | data formatting | bytes 4194304
  150.5 8.5 %collective-permute-start.5 = (bf16[1,256,256]{2,1,0:T(8,128)(2,1)S(1)}, bf16[1,256,256]{2,1,0:T(8,128)(2,1)S(1)}, u32[]{:S(2)}, u32[]{:S(2)}) collective-permute-start(bf16[1,256,256]{2,1,0:T(8,128)(2,1)S(1)} %bitcast.129), channel_id=1, source_target_pairs={{0,6},{1,7},{2,4},{3,5},{4,2},{5,3},{6,0},{7,1},{8,14},{9,15},{10,... | collective-permute-start | bytes 393224 | tf_op jit(solution)/shard_map/ppermute | solution.py:28
  164.4 2.9 collective-permute-start.8
  171.0 2.6 collective-permute-start.10
  175.0 6.1 %all-to-all-start.1 = ((bf16[16,2,32768]{2,1,0:T(2,128)(2,1)}), bf16[16,2,32768]{2,1,0:T(2,128)(2,1)}, u32[]{:S(2)}, u32[]{:S(2)}) async-start(bf16[16,2,32768]{2,1,0:T(2,128)(2,1)} %reshape.159), calls=%async_computation.1 | async-start | bytes 4194304 | tf_op jit(solution)/shard_map/all_to_all | solution.py:73
  186.9 10.0 %collective-permute-start.13 = (bf16[1,256,256]{2,1,0:T(8,128)(2,1)S(1)}, bf16[1,256,256]{2,1,0:T(8,128)(2,1)S(1)}, u32[]{:S(2)}, u32[]{:S(2)}) collective-permute-start(bf16[1,256,256]{2,1,0:T(8,128)(2,1)S(1)} %bitcast.116), channel_id=1, source_target_pairs={{0,14},{1,15},{2,12},{3,13},{4,10},{5,11},{6,8},{7,9},{8,6},{9,7},... | collective-permute-start | bytes 393224 | tf_op jit(solution)/shard_map/ppermute | solution.py:28
  202.2 48.8 %collective-permute-done.11 = bf16[1,256,256]{2,1,0:T(8,128)(2,1)S(1)} collective-permute-done((bf16[1,256,256]{2,1,0:T(8,128)(2,1)S(1)}, bf16[1,256,256]{2,1,0:T(8,128)(2,1)S(1)}, u32[]{:S(2)}, u32[]{:S(2)}) %collective-permute-start.11) | collective-permute-done | bytes 131104 | tf_op jit(solution)/shard_map/ppermute | solution.py:28
  262.3 5.5 %gather_fusion.1 = bf16[64,256,256]{2,1,0:T(8,128)(2,1)} fusion(bf16[16,256,256]{2,1,0:T(8,128)(2,1)S(1)} %gather_fusion, s32[1024]{0:T(1024)S(1)} %pad_clamp_fusion), kind=kCustom, calls=%fused_computation.clone | custom fusion | bytes 16777472 | tf_op jit(solution)/shard_map/while/body/eval_jaxpr/jit(_take)/gather | solution.py:39
  267.9 10.5 %reshape.158 = bf16[4096,1,256]{2,1,0:T(2,128)(2,1)} reshape(bf16[16,2,32768]{2,1,0:T(2,128)(2,1)} %copy-done) | data formatting | bytes 4194304
  278.3 3.9 copy.63
  282.2 2.8 copy.56
  285.1 5.5 %gather_fusion.2 = bf16[64,256,256]{2,1,0:T(8,128)(2,1)} fusion(bf16[16,256,256]{2,1,0:T(8,128)(2,1)S(1)} %bitcast.101, s32[1024]{0:T(1024)S(1)} %pad_clamp_fusion), kind=kCustom, calls=%fused_computation.1.clone | custom fusion | bytes 16777472 | tf_op jit(solution)/shard_map/while/body/eval_jaxpr/jit(_take)/gather | solution.py:38
  290.6 11.6 %broadcast_select_fusion = (bf16[64,256,256]{2,1,0:T(8,128)(2,1)}, bf16[64,256,256]{2,1,0:T(8,128)(2,1)}) fusion(bf16[64,256,256]{2,1,0:T(8,128)(2,1)} %gather_fusion.2, pred[64]{0:T(512)(128)(4,1)S(1)} %compare_and_fusion, bf16[64,256,256]{2,1,0:T(8,128)(2,1)} %gather_fusion.1), kind=kLoop, calls=%fused_computation.10 | loop fusion | flops 8388608 | bytes 33554496 | tf_op jit(solution)/shard_map/while/body/eval_jaxpr/jit(_take)/select_n | solution.py:38
  302.2 11.9 %copy.57 = bf16[64,256,256]{1,2,0:T(8,128)(2,1)} copy(bf16[64,256,256]{2,1,0:T(8,128)(2,1)} %get-tuple-element.40) | data formatting | bytes 16777216 | tf_op jit(solution)/shard_map/while/body/eval_jaxpr/jit(_take)/select_n | solution.py:38
  314.1 7.4 %reshape.160 = bf16[4096,4,64]{2,1,0:T(4,128)(2,1)} reshape(bf16[16,2,32768]{2,1,0:T(2,128)(2,1)} %all-to-all-done.1) | data formatting | bytes 4194304
  321.6 5.4 %copy.59 = bf16[4,64,16,256]{3,1,0,2:T(8,128)(2,1)S(1)} copy(bf16[4,64,16,256]{1,0,3,2:T(4,128)(2,1)} %bitcast.104) | data formatting | bytes 4194304 | tf_op jit(solution)/shard_map/all_to_all | solution.py:73
  326.9 3.3 reshape.115
  330.2 11.9 %copy.54 = bf16[64,256,256]{1,2,0:T(8,128)(2,1)} copy(bf16[64,256,256]{2,1,0:T(8,128)(2,1)} %get-tuple-element.41) | data formatting | bytes 16777216 | tf_op jit(solution)/shard_map/while/body/eval_jaxpr/jit(_take)/select_n | solution.py:39
  342.1 12.7 %fusion.6 = f32[64,4,256,64]{2,3,1,0:T(8,128)} fusion(bf16[64,256,4,64]{1,3,2,0:T(8,128)(2,1)} %bitcast.100, bf16[64,64,4,64]{3,2,1,0:T(4,128)(2,1)} %reshape.115), kind=kOutput, calls=%fused_computation.12 | convolution fusion | flops 536870912 | bytes 27262976 | tf_op jit(solution)/shard_map/while/body/eval_jaxpr/tihd,tjhd->thij/dot_general | solution.py:41
  354.8 14.7 %fusion.19 = f32[64,4,64]{2,1,0:T(4,128)S(1)} fusion(f32[64,4,256,64]{2,3,1,0:T(8,128)} %fusion.6), kind=kOutput, calls=%fused_computation.61 | output fusion | flops 8388863 | bytes 16842752 | tf_op jit(solution)/shard_map/while/body/eval_jaxpr/sub | solution.py:45
  369.5 43.2 %fusion.8 = bf16[64,4,64,64]{3,2,1,0:T(8,128)(2,1)} fusion(bf16[64,256,4,64]{1,3,2,0:T(8,128)(2,1)} %bitcast.108, f32[64,4,64]{2,1,0:T(4,128)S(1)} %fusion.19, f32[64,4,256,64]{2,3,1,0:T(8,128)} %fusion.6), kind=kOutput, calls=%fused_computation.14 | convolution fusion | flops 550519040 | bytes 27328512 | tf_op jit(solution)/shard_map/while/body/eval_jaxpr/thij,tjhd->tihd/dot_general | solution.py:47
  412.7 4.8 copy.61
  417.5 4.4 all-to-all-start.2
  422.1 47.3 %all-to-all-done.2 = bf16[64,64,256]{2,1,0:T(8,128)(2,1)S(1)} async-done(((bf16[64,64,256]{2,1,0:T(8,128)(2,1)}), bf16[64,64,256]{2,1,0:T(8,128)(2,1)S(1)}, u32[]{:S(2)}, u32[]{:S(2)}) %all-to-all-start.2) | async-done | bytes 2097184 | tf_op jit(solution)/shard_map/all_to_all | solution.py:75
  471.5 9.3 %convolution_convert_fusion = bf16[256,2048]{1,0:T(8,128)(2,1)} fusion(bf16[4096,2048]{1,0:T(8,128)(2,1)} %all-gather.3.cloned.1.call-done, bf16[256,4096]{1,0:T(8,128)(2,1)S(1)} %bitcast.114, pred[256]{0:T(512)(128)(4,1)S(1)} %lt.88), kind=kOutput, calls=%fused_computation.15 | convolution fusion | flops 4296540160 | bytes 19923200 | tf_op jit(solution)/shard_map/dot_general | solution.py:81
  (85 shorter events, 54.7 us)
Async XLA Ops:
  6.5 465.0 %all-gather.3.cloned.1.call-start = ((), (), s32[]{:S(2)}) async-start(), calls=%async_computation.3 | async-start | bytes 17825792 | tf_op jit(solution)/shard_map/all_gather | solution.py:83
  41.5 132.2 %all-to-all-start = ((bf16[16,2,32768]{2,1,0:T(2,128)(2,1)}), bf16[16,2,32768]{2,1,0:T(2,128)(2,1)S(1)}, u32[]{:S(2)}, u32[]{:S(2)}) async-start(bf16[16,2,32768]{2,1,0:T(2,128)(2,1)} %reshape.157), calls=%async_computation | async-start | bytes 4194304 | tf_op jit(solution)/shard_map/all_to_all | solution.py:70
  52.1 15.4 %copy-start.3 = (u32[32]{0:T(128)S(1)}, u32[32]{0:T(128)}, u32[]{:S(2)}) copy-start(u32[32]{0:T(128)} %constant.76) | copy-start | bytes 388
  52.1 16.7 %copy-start.1 = (s32[4,1]{0,1:T(1,128)S(1)}, s32[4,1]{0,1:T(1,128)}, u32[]{:S(2)}) copy-start(s32[4,1]{0,1:T(1,128)} %param.12) | copy-start | bytes 52
  56.3 94.2 %collective-permute-start = (bf16[1,256,256]{2,1,0:T(8,128)(2,1)}, bf16[1,256,256]{2,1,0:T(8,128)(2,1)}, u32[]{:S(2)}, u32[]{:S(2)}) collective-permute-start(bf16[1,256,256]{2,1,0:T(8,128)(2,1)} %bitcast.128), channel_id=1, source_target_pairs={{0,1},{1,0},{2,3},{3,2},{4,5},{5,4},{6,7},{7,6},{8,9},{9,8},{10,11... | collective-permute-start | bytes 393224 | tf_op jit(solution)/shard_map/ppermute | solution.py:28
  58.3 102.2 %collective-permute-start.1 = (bf16[1,256,256]{2,1,0:T(8,128)(2,1)}, bf16[1,256,256]{2,1,0:T(8,128)(2,1)}, u32[]{:S(2)}, u32[]{:S(2)}) collective-permute-start(bf16[1,256,256]{2,1,0:T(8,128)(2,1)} %bitcast.127), channel_id=1, source_target_pairs={{0,2},{1,3},{2,0},{3,1},{4,6},{5,7},{6,4},{7,5},{8,10},{9,11},{10,... | collective-permute-start | bytes 393224 | tf_op jit(solution)/shard_map/ppermute | solution.py:28
  60.3 102.5 %collective-permute-start.2 = (bf16[1,256,256]{2,1,0:T(8,128)(2,1)}, bf16[1,256,256]{2,1,0:T(8,128)(2,1)}, u32[]{:S(2)}, u32[]{:S(2)}) collective-permute-start(bf16[1,256,256]{2,1,0:T(8,128)(2,1)} %bitcast.126), channel_id=1, source_target_pairs={{0,3},{1,2},{2,1},{3,0},{4,7},{5,6},{6,5},{7,4},{8,11},{9,10},{10,... | collective-permute-start | bytes 393224 | tf_op jit(solution)/shard_map/ppermute | solution.py:28
  63.4 101.0 %collective-permute-start.3 = (bf16[1,256,256]{2,1,0:T(8,128)(2,1)}, bf16[1,256,256]{2,1,0:T(8,128)(2,1)}, u32[]{:S(2)}, u32[]{:S(2)}) collective-permute-start(bf16[1,256,256]{2,1,0:T(8,128)(2,1)} %bitcast.124), channel_id=1, source_target_pairs={{0,4},{1,5},{2,6},{3,7},{4,0},{5,1},{6,2},{7,3},{8,12},{9,13},{10,... | collective-permute-start | bytes 393224 | tf_op jit(solution)/shard_map/ppermute | solution.py:28
  65.4 103.5 %collective-permute-start.4 = (bf16[1,256,256]{2,1,0:T(8,128)(2,1)}, bf16[1,256,256]{2,1,0:T(8,128)(2,1)}, u32[]{:S(2)}, u32[]{:S(2)}) collective-permute-start(bf16[1,256,256]{2,1,0:T(8,128)(2,1)} %bitcast.123), channel_id=1, source_target_pairs={{0,5},{1,4},{2,7},{3,6},{4,1},{5,0},{6,3},{7,2},{8,13},{9,12},{10,... | collective-permute-start | bytes 393224 | tf_op jit(solution)/shard_map/ppermute | solution.py:28
  150.5 20.6 %collective-permute-start.5 = (bf16[1,256,256]{2,1,0:T(8,128)(2,1)S(1)}, bf16[1,256,256]{2,1,0:T(8,128)(2,1)S(1)}, u32[]{:S(2)}, u32[]{:S(2)}) collective-permute-start(bf16[1,256,256]{2,1,0:T(8,128)(2,1)S(1)} %bitcast.129), channel_id=1, source_target_pairs={{0,6},{1,7},{2,4},{3,5},{4,2},{5,3},{6,0},{7,1},{8,14},{9,15},{10,... | collective-permute-start | bytes 393224 | tf_op jit(solution)/shard_map/ppermute | solution.py:28
  160.5 21.3 %collective-permute-start.6 = (bf16[1,256,256]{2,1,0:T(8,128)(2,1)S(1)}, bf16[1,256,256]{2,1,0:T(8,128)(2,1)}, u32[]{:S(2)}, u32[]{:S(2)}) collective-permute-start(bf16[1,256,256]{2,1,0:T(8,128)(2,1)S(1)} %bitcast.125), channel_id=1, source_target_pairs={{0,7},{1,6},{2,5},{3,4},{4,3},{5,2},{6,1},{7,0},{8,15},{9,14},{10,... | collective-permute-start | bytes 393224 | tf_op jit(solution)/shard_map/ppermute | solution.py:28
  162.8 21.8 %collective-permute-start.7 = (bf16[1,256,256]{2,1,0:T(8,128)(2,1)S(1)}, bf16[1,256,256]{2,1,0:T(8,128)(2,1)}, u32[]{:S(2)}, u32[]{:S(2)}) collective-permute-start(bf16[1,256,256]{2,1,0:T(8,128)(2,1)S(1)} %bitcast.122), channel_id=1, source_target_pairs={{0,8},{1,9},{2,10},{3,11},{4,12},{5,13},{6,14},{7,15},{8,0},{9,1},... | collective-permute-start | bytes 393224 | tf_op jit(solution)/shard_map/ppermute | solution.py:28
  164.4 22.5 %collective-permute-start.8 = (bf16[1,256,256]{2,1,0:T(8,128)(2,1)S(1)}, bf16[1,256,256]{2,1,0:T(8,128)(2,1)}, u32[]{:S(2)}, u32[]{:S(2)}) collective-permute-start(bf16[1,256,256]{2,1,0:T(8,128)(2,1)S(1)} %bitcast.121), channel_id=1, source_target_pairs={{0,9},{1,8},{2,11},{3,10},{4,13},{5,12},{6,15},{7,14},{8,1},{9,0},... | collective-permute-start | bytes 393224 | tf_op jit(solution)/shard_map/ppermute | solution.py:28
  168.9 29.7 %collective-permute-start.9 = (bf16[1,256,256]{2,1,0:T(8,128)(2,1)S(1)}, bf16[1,256,256]{2,1,0:T(8,128)(2,1)}, u32[]{:S(2)}, u32[]{:S(2)}) collective-permute-start(bf16[1,256,256]{2,1,0:T(8,128)(2,1)S(1)} %bitcast.120), channel_id=1, source_target_pairs={{0,10},{1,11},{2,8},{3,9},{4,14},{5,15},{6,12},{7,13},{8,2},{9,3},... | collective-permute-start | bytes 393224 | tf_op jit(solution)/shard_map/ppermute | solution.py:28
  171.0 30.5 %collective-permute-start.10 = (bf16[1,256,256]{2,1,0:T(8,128)(2,1)S(1)}, bf16[1,256,256]{2,1,0:T(8,128)(2,1)S(1)}, u32[]{:S(2)}, u32[]{:S(2)}) collective-permute-start(bf16[1,256,256]{2,1,0:T(8,128)(2,1)S(1)} %bitcast.119), channel_id=1, source_target_pairs={{0,11},{1,10},{2,9},{3,8},{4,15},{5,14},{6,13},{7,12},{8,3},{9,2},... | collective-permute-start | bytes 393224 | tf_op jit(solution)/shard_map/ppermute | solution.py:28
  173.7 1.3 copy-start
  175.0 139.1 %all-to-all-start.1 = ((bf16[16,2,32768]{2,1,0:T(2,128)(2,1)}), bf16[16,2,32768]{2,1,0:T(2,128)(2,1)}, u32[]{:S(2)}, u32[]{:S(2)}) async-start(bf16[16,2,32768]{2,1,0:T(2,128)(2,1)} %reshape.159), calls=%async_computation.1 | async-start | bytes 4194304 | tf_op jit(solution)/shard_map/all_to_all | solution.py:73
  181.8 69.2 %collective-permute-start.11 = (bf16[1,256,256]{2,1,0:T(8,128)(2,1)S(1)}, bf16[1,256,256]{2,1,0:T(8,128)(2,1)S(1)}, u32[]{:S(2)}, u32[]{:S(2)}) collective-permute-start(bf16[1,256,256]{2,1,0:T(8,128)(2,1)S(1)} %bitcast.118), channel_id=1, source_target_pairs={{0,12},{1,13},{2,14},{3,15},{4,8},{5,9},{6,10},{7,11},{8,4},{9,5},... | collective-permute-start | bytes 393224 | tf_op jit(solution)/shard_map/ppermute | solution.py:28
  184.6 69.2 %collective-permute-start.12 = (bf16[1,256,256]{2,1,0:T(8,128)(2,1)S(1)}, bf16[1,256,256]{2,1,0:T(8,128)(2,1)S(1)}, u32[]{:S(2)}, u32[]{:S(2)}) collective-permute-start(bf16[1,256,256]{2,1,0:T(8,128)(2,1)S(1)} %bitcast.117), channel_id=1, source_target_pairs={{0,13},{1,12},{2,15},{3,14},{4,9},{5,8},{6,11},{7,10},{8,5},{9,4},... | collective-permute-start | bytes 393224 | tf_op jit(solution)/shard_map/ppermute | solution.py:28
  186.9 69.7 %collective-permute-start.13 = (bf16[1,256,256]{2,1,0:T(8,128)(2,1)S(1)}, bf16[1,256,256]{2,1,0:T(8,128)(2,1)S(1)}, u32[]{:S(2)}, u32[]{:S(2)}) collective-permute-start(bf16[1,256,256]{2,1,0:T(8,128)(2,1)S(1)} %bitcast.116), channel_id=1, source_target_pairs={{0,14},{1,15},{2,12},{3,13},{4,10},{5,11},{6,8},{7,9},{8,6},{9,7},... | collective-permute-start | bytes 393224 | tf_op jit(solution)/shard_map/ppermute | solution.py:28
  198.5 60.9 %collective-permute-start.14 = (bf16[1,256,256]{2,1,0:T(8,128)(2,1)S(1)}, bf16[1,256,256]{2,1,0:T(8,128)(2,1)S(1)}, u32[]{:S(2)}, u32[]{:S(2)}) collective-permute-start(bf16[1,256,256]{2,1,0:T(8,128)(2,1)S(1)} %bitcast.115), channel_id=1, source_target_pairs={{0,15},{1,14},{2,13},{3,12},{4,11},{5,10},{6,9},{7,8},{8,7},{9,6},... | collective-permute-start | bytes 393224 | tf_op jit(solution)/shard_map/ppermute | solution.py:28
  417.5 4.4 copy-start.2
  417.5 51.9 %all-to-all-start.2 = ((bf16[64,64,256]{2,1,0:T(8,128)(2,1)}), bf16[64,64,256]{2,1,0:T(8,128)(2,1)S(1)}, u32[]{:S(2)}, u32[]{:S(2)}) async-start(bf16[64,64,256]{2,1,0:T(8,128)(2,1)} %copy.61), calls=%async_computation.2 | async-start | bytes 4194304 | tf_op jit(solution)/shard_map/all_to_all | solution.py:75
Sparse Core Ops, SparseCore 0:
  9.5 173.0 all-gather.2
